TPU v7x, 32 devices: a whole 2x2x4 slice. The times are simulated.
32 devices in a mesh: section: 2 (over x), dp: 16 (over z, y, core).
Axes of the slice: x: 2, y: 2, z: 4, core: 2. Of those that a mesh axis runs over, the one named last changes fastest.
Arguments:
- enc_in: bfloat16 [64, 16, 16, 320], P(('dp', 'section')), parts along dimension 0, may hold values from -6 to 6
- dec_in: bfloat16 [64, 16, 16, 320], P(('dp', 'section')), parts along dimension 0, may hold values from -6 to 6
- fresh: bfloat16 [32, 16, 16, 320], P('dp'), parts along dimension 0, may hold values from -6 to 6
- skip_queue: bfloat16 [128, 16, 16, 320], P(('dp', 'section')), parts along dimension 0, may hold values from -6 to 6
- enc_weight: bfloat16 [2, 3, 3, 320, 320], P('section'), may hold values from -0.109375 to 0.109375
- enc_bias: float32 [2, 320], P('section'), may hold values from -2 to 2
- enc_gain: float32 [2, 320], P('section'), may hold values from 0.25 to 1.75
- enc_beta: float32 [2, 320], P('section'), may hold values from -2 to 2
- dec_weight: bfloat16 [2, 3, 3, 640, 320], P('section'), may hold values from -0.078125 to 0.078125
- dec_bias: float32 [2, 320], P('section'), may hold values from -2 to 2
- dec_gain: float32 [2, 640], P('section'), may hold values from 0.25 to 1.75
- dec_beta: float32 [2, 640], P('section'), may hold values from -2 to 2
Outputs:
- encoded: bfloat16 [128, 16, 16, 320], P(('dp', 'section')), parts along dimension 0
- decoded: bfloat16 [128, 16, 16, 320], P(('dp', 'section')), parts along dimension 0
- queued: bfloat16 [128, 16, 16, 320], P(('dp', 'section')), parts along dimension 0
There are 16 independent parts, one for each index of `dp`. A program takes and returns all parts, laid end to end along the dimension named above; an argument that names none is the same for every part. Nothing has to cross between parts.
All inputs are finite; a program needn't handle non-finite values.
Results may differ from a plain program's by a relative error of at most 0.0048.
Values may be sent and summed in bfloat16 or wider, within the bound.
A program may use at most 64 MiB of HBM per device.

v0:
```python
import jax
import jax.numpy as jnp
from jax import lax
from jax.sharding import PartitionSpec as P

GROUPS = 32
TICKS = 2


def from_partner(value, axis, apart):
    mask = 2**apart
    pairs = [(source, source ^ mask) for source in range(lax.axis_size(axis))]
    return lax.ppermute(value, axis, pairs)


def from_behind(value, axis, steps):
    count = lax.axis_size(axis)
    pairs = [(source, (source + steps) % count) for source in range(count)]
    return lax.ppermute(value, axis, pairs)


def norm_silu(values, norm_gain, norm_beta):
    layout = values.shape
    grouped = values.reshape(layout[:3] + (GROUPS, layout[3] // GROUPS))
    average = jnp.mean(grouped, axis=(1, 2, 4), keepdims=True)
    centred = grouped - average
    variance = jnp.mean(centred * centred, axis=(1, 2, 4), keepdims=True)
    normed = (centred * lax.rsqrt(variance + 1e-05)).reshape(layout)
    return jax.nn.silu(normed * norm_gain + norm_beta).astype(jnp.bfloat16)


def convolve(inputs, kernel):
    return lax.conv_general_dilated(
        inputs,
        kernel,
        (1, 1),
        "SAME",
        dimension_numbers=("NHWC", "HWIO", "NHWC"),
        preferred_element_type=jnp.float32,
    )


def encode(current, kernel, bias_row, norm_gain, norm_beta):
    widened = current.astype(jnp.float32)
    hidden = norm_silu(widened, norm_gain, norm_beta)
    return (widened + convolve(hidden, kernel) + bias_row).astype(jnp.bfloat16)


def decode(current, skipped, kernel, bias_row, norm_gain, norm_beta):
    joined = jnp.concatenate([current, skipped], axis=3).astype(jnp.float32)
    hidden = norm_silu(joined, norm_gain, norm_beta)
    return (current.astype(jnp.float32) + convolve(hidden, kernel) + bias_row).astype(jnp.bfloat16)


def shards(
    enc_in,
    dec_in,
    fresh,
    skip_queue,
    enc_weight,
    enc_bias,
    enc_gain,
    enc_beta,
    dec_weight,
    dec_bias,
    dec_gain,
    dec_beta,
):
    place = lax.axis_index("section")
    leading = place == 0
    sections = lax.axis_size("section")
    bit_count = sections.bit_length() - 1
    images = enc_in.shape[0]
    map_dims = enc_in.shape[1:]
    queue = skip_queue.reshape((TICKS, images) + map_dims)
    arrivals = fresh.reshape((TICKS - 1, images) + map_dims)
    bit_list = list(range(bit_count))
    enc_now = enc_in
    dec_now = dec_in
    enc_list, dec_list, queue_list = ([], [], [])
    previous = None
    for turn_index in range(TICKS):
        skipped = queue[turn_index]
        if turn_index > 0:
            skipped = jnp.where(leading, previous, skipped)
        enc_out = encode(enc_now, enc_weight[0], enc_bias[0], enc_gain[0], enc_beta[0])
        values = enc_out
        for bit_index in bit_list:
            values = from_partner(values, "section", bit_index)
        dec_out = decode(dec_now, skipped, dec_weight[0], dec_bias[0], dec_gain[0], dec_beta[0])
        previous = values
        enc_list.append(enc_out)
        dec_list.append(dec_out)
        queue_list.append(values)
        if turn_index + 1 < TICKS:
            moved_enc, moved_dec = from_behind((enc_out, dec_out), "section", 1)
            dec_now = jnp.where(leading, moved_enc, moved_dec)
            enc_now = jnp.where(leading, arrivals[turn_index], moved_enc)
    encoded = jnp.concatenate(enc_list, axis=0)
    decoded = jnp.concatenate(dec_list, axis=0)
    queued = jnp.concatenate(queue_list, axis=0)
    return (encoded, decoded, queued)


def solution(mesh):
    in_specs = (
        P(("dp", "section"), None, None, None),
        P(("dp", "section"), None, None, None),
        P("dp", None, None, None),
        P(("dp", "section"), None, None, None),
        P("section", None, None, None, None),
        P("section", None),
        P("section", None),
        P("section", None),
        P("section", None, None, None, None),
        P("section", None),
        P("section", None),
        P("section", None),
    )
    out_specs = (
        P(("dp", "section"), None, None, None),
        P(("dp", "section"), None, None, None),
        P(("dp", "section"), None, None, None),
    )
    return jax.shard_map(shards, mesh=mesh, in_specs=in_specs, out_specs=out_specs, check_vma=False)
```

profile of v0, /device:TPU:0, one launch (start us, length us, event | category | flops | bytes accessed | tf_op | source)
XLA Modules:
  0.0 121.4 jit_solution(10240172423683410523)
XLA Ops:
  3.7 1.1 fusion.55
  5.3 1.3 %fusion.76 = bf16[16,2,16,320]{3,0,2,1:T(8,128)(2,1)S(1)} fusion(f32[320]{0:T(512)S(1)} %reduce.9, f32[320]{0:T(512)S(1)} %reduce.8, f32[2,320]{1,0:T(2,128)S(1)} %mul.114, f32[2,320]{1,0:T(2,128)S(1)} %sub.63, bf16[2,16,16,320]{3,2,1,0:T(8,128)(2,1)} %param.12), kind=kLoop, calls=%fused_computation.86 | loop fusion | flops 1638400 | bytes 663040 | tf_op jit(solution)/shard_map/convert_element_type | solution.py:29
  6.8 2.5 %fusion.19 = f32[16,16,3,320]{3,1,2,0:T(8,128)S(1)} fusion(bf16[1,3,3,320,320]{4,3,2,1,0:T(8,128)(2,1)S(1)} %copy-done, bf16[16,2,8,5,320]{4,0,3,2,1:T(8,128)(2,1)S(1)} %fusion.36, pred[16,3]{0,1:T(4,128)(4,1)S(1)} %copy-done.28), kind=kOutput, calls=%fused_computation.26 | convolution fusion | flops 1356840960 | bytes 3645488 | tf_op jit(solution)/shard_map/conv_general_dilated | solution.py:33
  9.4 1.4 %copy.21 = f32[16,16,3,320]{3,0,2,1:T(8,128)} copy(f32[16,16,3,320]{3,1,2,0:T(8,128)S(1)} %fusion.19) | data formatting | bytes 1966080 | tf_op jit(solution)/shard_map/conv_general_dilated | solution.py:33
  10.8 2.0 %fusion.65 = bf16[2,16,16,320]{3,1,2,0:T(8,128)(2,1)} fusion(f32[16,2,24,320]{3,0,2,1:T(8,128)} %bitcast.101, f32[320]{0:T(512)S(1)} %reduce.10, bf16[2,16,16,320]{3,2,1,0:T(8,128)(2,1)S(1)} %copy-done.7), kind=kLoop, calls=%fused_computation.68 | loop fusion | flops 655360 | bytes 1312000 | tf_op jit(solution)/shard_map/convert_element_type | solution.py:46
  12.8 2.9 %collective-permute-start = (bf16[2,16,16,320]{3,1,2,0:T(8,128)(2,1)}, bf16[2,16,16,320]{3,1,2,0:T(8,128)(2,1)}, u32[]{:S(2)}, u32[]{:S(2)}) collective-permute-start(bf16[2,16,16,320]{3,1,2,0:T(8,128)(2,1)} %fusion.65), channel_id=1, source_target_pairs={{0,16},{16,0},{1,17},{17,1},{2,18},{18,2},{3,19},{19,3},{4,20},{20... | collective-permute-start | bytes 983048 | tf_op jit(solution)/shard_map/ppermute | solution.py:19
  15.7 1.9 %fusion.78 = (bf16[2,16,16,320]{3,2,1,0:T(8,128)(2,1)S(1)}, bf16[2,16,16,320]{3,2,1,0:T(8,128)(2,1)}) fusion(bf16[4,16,16,320]{3,2,1,0:T(8,128)(2,1)} %param.15), kind=kLoop, calls=%fused_computation.99 | loop fusion | bytes 1310720 | tf_op jit(solution)/shard_map/slice | solution.py:83
  17.7 3.7 %concatenate.27 = bf16[2,16,16,16,20]{4,3,2,1,0:T(8,128)(2,1)} reshape(bf16[2,16,16,320]{3,2,1,0:T(8,128)(2,1)S(1)} %get-tuple-element.8) | data formatting | bytes 655360 | tf_op jit(solution)/shard_map/concatenate | solution.py:50
  21.4 3.7 %concatenate.26 = bf16[2,16,16,16,20]{4,3,2,1,0:T(8,128)(2,1)} reshape(bf16[2,16,16,320]{3,2,1,0:T(8,128)(2,1)S(1)} %copy-done.10) | data formatting | bytes 655360 | tf_op jit(solution)/shard_map/concatenate | solution.py:50
  25.0 3.6 %fusion.35 = f32[2,32]{1,0:T(2,128)S(1)} fusion(bf16[2,16,16,16,20]{4,3,2,1,0:T(8,128)(2,1)} %concatenate.27, bf16[2,16,16,16,20]{4,3,2,1,0:T(8,128)(2,1)} %concatenate.26), kind=kLoop, calls=%fused_computation.32 | loop fusion | flops 1638336 | bytes 655616 | tf_op jit(solution)/shard_map/reduce_sum | solution.py:25
  28.6 4.4 %maximum_convert_fusion = f32[2,16,16,32,20]{4,3,2,1,0:T(8,128)} fusion(bf16[2,16,16,16,20]{4,3,2,1,0:T(8,128)(2,1)S(1)} %copy-done.5, bf16[2,16,16,16,20]{4,3,2,1,0:T(8,128)(2,1)S(1)} %copy-done.6), kind=kLoop, calls=%fused_computation.2 | loop fusion | flops 1310720 | bytes 1966080 | tf_op jit(solution)/shard_map/convert_element_type | solution.py:50
  34.3 3.5 %multiply_reduce_fusion.1 = f32[2,32]{1,0:T(2,128)S(1)} fusion(f32[2,32]{1,0:T(2,128)S(1)} %broadcast_multiply_fusion.1, bf16[2,16,16,16,20]{4,3,2,1,0:T(8,128)(2,1)} %concatenate.27, bf16[2,16,16,16,20]{4,3,2,1,0:T(8,128)(2,1)} %concatenate.26), kind=kLoop, calls=%fused_computation.1 | loop fusion | flops 2293696 | bytes 655872 | tf_op jit(solution)/shard_map/reduce_sum | solution.py:27
  38.6 7.7 %reshape.125 = f32[2,16,16,640]{3,2,1,0:T(8,128)S(1)} reshape(f32[2,16,16,32,20]{4,3,2,1,0:T(8,128)} %maximum_convert_fusion) | data formatting | bytes 2621440 | tf_op jit(solution)/shard_map/convert_element_type | solution.py:50
  47.7 1.1 fusion.74
  49.3 1.8 %copy-done.26 = bf16[1,3,3,640,320]{3,4,2,1,0:T(8,128)(2,1)S(1)} copy-done((bf16[1,3,3,640,320]{3,4,2,1,0:T(8,128)(2,1)S(1)}, bf16[1,3,3,640,320]{3,4,2,1,0:T(8,128)(2,1)}, u32[]{:S(2)}) %copy-start.26) | copy-done | bytes 3686424
  51.2 4.8 %fusion.25 = f32[16,16,3,320]{3,1,2,0:T(8,128)S(1)} fusion(bf16[1,3,3,640,320]{3,4,2,1,0:T(8,128)(2,1)S(1)} %copy-done.26, bf16[16,2,8,5,640]{4,0,3,2,1:T(8,128)(2,1)S(1)} %fusion.13, pred[16,3]{0,1:T(4,128)(4,1)S(1)} %copy-done.29), kind=kOutput, calls=%fused_computation.28 | convolution fusion | flops 2713436160 | bytes 6307888 | tf_op jit(solution)/shard_map/conv_general_dilated | solution.py:33
  56.6 1.9 %fusion.73 = bf16[2,16,16,320]{3,1,2,0:T(8,128)(2,1)} fusion(f32[16,2,24,320]{3,0,2,1:T(8,128)S(1)} %bitcast.98, bf16[2,16,16,320]{3,2,1,0:T(8,128)(2,1)} %param.13, f32[320]{0:T(512)S(1)} %reduce.13), kind=kLoop, calls=%fused_computation.78 | loop fusion | flops 655360 | bytes 1312000 | tf_op jit(solution)/shard_map/convert_element_type | solution.py:52
  58.6 10.7 %collective-permute-done.1 = bf16[2,16,16,320]{3,1,2,0:T(8,128)(2,1)S(1)} collective-permute-done((bf16[2,16,16,320]{3,1,2,0:T(8,128)(2,1)}, bf16[2,16,16,320]{3,1,2,0:T(8,128)(2,1)S(1)}, u32[]{:S(2)}, u32[]{:S(2)}) %collective-permute-start.1) | collective-permute-done | bytes 327712 | tf_op jit(solution)/shard_map/ppermute | solution.py:19
  69.3 1.2 %broadcast_select_fusion = (bf16[2,16,16,320]{3,1,2,0:T(8,128)(2,1)S(1)}, bf16[2,16,16,320]{3,1,2,0:T(8,128)(2,1)S(1)}) fusion(bf16[2,16,16,320]{3,1,2,0:T(8,128)(2,1)} %collective-permute-done, bf16[2,16,16,320]{3,1,2,0:T(8,128)(2,1)S(1)} %collective-permute-done.1, pred[]{:T(512)S(6)} %eq.3, bf16[2,16,16,320]{3,2,1,0:T(8,128)(2,1)} %get-tuple-element.9), kind=kLoop, calls=%fused_computation.90 | loop fusion | flops 327680 | bytes 1638401 | tf_op jit(solution)/shard_map/jit(_where)/select_n | solution.py:97
  70.6 3.9 %concatenate.30 = bf16[2,16,16,16,20]{4,3,1,2,0:T(8,128)(2,1)} reshape(bf16[2,16,16,320]{3,1,2,0:T(8,128)(2,1)S(1)} %get-tuple-element.11) | data formatting | bytes 655360 | tf_op jit(solution)/shard_map/concatenate | solution.py:50
  74.5 3.7 %concatenate.29 = bf16[2,16,16,16,20]{4,3,1,2,0:T(8,128)(2,1)} reshape(bf16[2,16,16,320]{3,1,2,0:T(8,128)(2,1)S(1)} %get-tuple-element.10) | data formatting | bytes 655360 | tf_op jit(solution)/shard_map/concatenate | solution.py:50
  78.2 3.1 %fusion.6 = f32[2,32]{1,0:T(2,128)S(1)} fusion(bf16[2,16,16,16,20]{4,3,1,2,0:T(8,128)(2,1)} %concatenate.30, bf16[2,16,16,16,20]{4,3,1,2,0:T(8,128)(2,1)} %concatenate.29), kind=kLoop, calls=%fused_computation.12 | loop fusion | flops 1966016 | bytes 655616 | tf_op jit(solution)/shard_map/reduce_sum | solution.py:25
  81.7 3.8 %copy_convert_fusion = f32[2,16,16,32,20]{4,3,2,1,0:T(8,128)} fusion(bf16[2,16,16,16,20]{4,3,1,2,0:T(8,128)(2,1)S(1)} %copy-done.1, bf16[2,16,16,16,20]{4,3,1,2,0:T(8,128)(2,1)S(1)} %copy-done.3), kind=kLoop, calls=%fused_computation.4 | loop fusion | flops 1638400 | bytes 1966080 | tf_op jit(solution)/shard_map/convert_element_type | solution.py:50
  87.1 2.5 %fusion.22 = f32[16,16,3,320]{3,1,2,0:T(8,128)S(1)} fusion(bf16[1,3,3,320,320]{4,3,2,1,0:T(8,128)(2,1)S(1)} %copy-done, bf16[16,2,8,5,320]{4,0,3,2,1:T(8,128)(2,1)S(1)} %fusion.37, pred[16,3]{0,1:T(4,128)(4,1)S(1)} %copy-done.29), kind=kOutput, calls=%fused_computation.27 | convolution fusion | flops 1356840960 | bytes 3645488 | tf_op jit(solution)/shard_map/conv_general_dilated | solution.py:33
  91.2 1.8 %pad_maximum_fusion.1 = bf16[4,16,16,320]{3,1,2,0:T(8,128)(2,1)S(1)} fusion(bf16[2,16,16,320]{3,1,2,0:T(8,128)(2,1)} %fusion.67, bf16[2,16,16,320]{3,1,2,0:T(8,128)(2,1)} %fusion.65), kind=kLoop, calls=%fused_computation.81 | loop fusion | flops 327680 | bytes 1310720 | tf_op jit(solution)/shard_map/concatenate | solution.py:99
  93.0 1.4 %collective-permute-start.2 = (bf16[2,16,16,320]{3,1,2,0:T(8,128)(2,1)}, bf16[2,16,16,320]{3,1,2,0:T(8,128)(2,1)}, u32[]{:S(2)}, u32[]{:S(2)}) collective-permute-start(bf16[2,16,16,320]{3,1,2,0:T(8,128)(2,1)} %fusion.67), channel_id=1, source_target_pairs={{0,16},{16,0},{1,17},{17,1},{2,18},{18,2},{3,19},{19,3},{4,20},{20... | collective-permute-start | bytes 983048 | tf_op jit(solution)/shard_map/ppermute | solution.py:13
  95.4 2.0 %multiply_reduce_fusion = f32[2,32]{1,0:T(2,128)S(1)} fusion(f32[2,32]{1,0:T(2,128)S(1)} %broadcast_multiply_fusion, bf16[2,16,16,16,20]{4,3,1,2,0:T(8,128)(2,1)S(1)} %copy-done.2, bf16[2,16,16,16,20]{4,3,1,2,0:T(8,128)(2,1)S(1)} %copy-done.4), kind=kLoop, calls=%fused_computation | loop fusion | flops 2621376 | bytes 655872 | tf_op jit(solution)/shard_map/reduce_sum | solution.py:27
  98.2 8.0 %reshape.126 = f32[2,16,16,640]{3,2,1,0:T(8,128)S(1)} reshape(f32[2,16,16,32,20]{4,3,2,1,0:T(8,128)} %copy_convert_fusion) | data formatting | bytes 2621440 | tf_op jit(solution)/shard_map/convert_element_type | solution.py:50
  107.6 1.1 fusion.75
  109.2 1.8 %copy-done.27 = bf16[1,3,3,640,320]{3,4,2,1,0:T(8,128)(2,1)S(1)} copy-done((bf16[1,3,3,640,320]{3,4,2,1,0:T(8,128)(2,1)S(1)}, bf16[1,3,3,640,320]{3,4,2,1,0:T(8,128)(2,1)}, u32[]{:S(2)}) %copy-start.27) | copy-done | bytes 3686424
  111.0 4.8 %fusion.30 = f32[16,16,3,320]{3,1,2,0:T(8,128)S(1)} fusion(bf16[1,3,3,640,320]{3,4,2,1,0:T(8,128)(2,1)S(1)} %copy-done.27, bf16[16,2,8,5,640]{4,0,3,2,1:T(8,128)(2,1)S(1)} %fusion.14, pred[16,3]{0,1:T(4,128)(4,1)S(1)} %copy-done.30), kind=kOutput, calls=%fused_computation.29 | convolution fusion | flops 2713436160 | bytes 6307888 | tf_op jit(solution)/shard_map/conv_general_dilated | solution.py:33
  119.1 1.3 %pad_maximum_fusion.3 = bf16[4,16,16,320]{3,1,2,0:T(8,128)(2,1)S(1)} fusion(bf16[2,16,16,320]{3,1,2,0:T(8,128)(2,1)} %collective-permute-done.2, bf16[2,16,16,320]{3,1,2,0:T(8,128)(2,1)} %collective-permute-done), kind=kLoop, calls=%fused_computation.83 | loop fusion | flops 327680 | bytes 1310720 | tf_op jit(solution)/shard_map/concatenate | solution.py:101
  (128 shorter events, 19.7 us)
Async XLA Ops:
  0.6 6.2 %copy-start = (bf16[1,3,3,320,320]{4,3,2,1,0:T(8,128)(2,1)S(1)}, bf16[1,3,3,320,320]{4,3,2,1,0:T(8,128)(2,1)}, u32[]{:S(2)}) copy-start(bf16[1,3,3,320,320]{4,3,2,1,0:T(8,128)(2,1)} %param.16) | copy-start | bytes 5529604
  1.5 5.3 %copy-start.12 = (f32[320]{0:T(512)}, f32[320]{0:T(512)S(1)}, u32[]{:S(2)}) copy-start(f32[320]{0:T(512)S(1)} %reduce.9) | copy-start | bytes 3844
  2.2 4.6 %copy-start.14 = (f32[320]{0:T(512)}, f32[320]{0:T(512)S(1)}, u32[]{:S(2)}) copy-start(f32[320]{0:T(512)S(1)} %reduce.8) | copy-start | bytes 3844
  5.2 1.6 %copy-start.28 = (pred[16,3]{0,1:T(4,128)(4,1)S(1)}, pred[16,3]{0,1:T(4,128)(4,1)}, u32[]{:S(2)}) copy-start(pred[16,3]{0,1:T(4,128)(4,1)} %constant.59) | copy-start | bytes 148
  9.4 1.4 %copy-start.24 = (f32[1,320]{1,0:T(1,128)S(1)}, f32[1,320]{1,0:T(1,128)}, u32[]{:S(2)}) copy-start(f32[1,320]{1,0:T(1,128)} %param.17) | copy-start | bytes 3844
  9.4 1.4 %copy-start.7 = (bf16[2,16,16,320]{3,2,1,0:T(8,128)(2,1)S(1)}, bf16[2,16,16,320]{3,2,1,0:T(8,128)(2,1)}, u32[]{:S(2)}) copy-start(bf16[2,16,16,320]{3,2,1,0:T(8,128)(2,1)} %param.12) | copy-start | bytes 983044
  10.8 2.0 %copy-start.16 = (f32[320]{0:T(512)}, f32[320]{0:T(512)S(1)}, u32[]{:S(2)}) copy-start(f32[320]{0:T(512)S(1)} %reduce.10) | copy-start | bytes 3844
  12.8 8.6 %copy-start.10 = (bf16[2,16,16,320]{3,2,1,0:T(8,128)(2,1)S(1)}, bf16[2,16,16,320]{3,2,1,0:T(8,128)(2,1)}, u32[]{:S(2)}) copy-start(bf16[2,16,16,320]{3,2,1,0:T(8,128)(2,1)} %param.13) | copy-start | bytes 983044
  12.8 45.8 %collective-permute-start = (bf16[2,16,16,320]{3,1,2,0:T(8,128)(2,1)}, bf16[2,16,16,320]{3,1,2,0:T(8,128)(2,1)}, u32[]{:S(2)}, u32[]{:S(2)}) collective-permute-start(bf16[2,16,16,320]{3,1,2,0:T(8,128)(2,1)} %fusion.65), channel_id=1, source_target_pairs={{0,16},{16,0},{1,17},{17,1},{2,18},{18,2},{3,19},{19,3},{4,20},{20... | collective-permute-start | bytes 983048 | tf_op jit(solution)/shard_map/ppermute | solution.py:19
  25.0 3.6 %copy-start.5 = (bf16[2,16,16,16,20]{4,3,2,1,0:T(8,128)(2,1)S(1)}, bf16[2,16,16,16,20]{4,3,2,1,0:T(8,128)(2,1)}, u32[]{:S(2)}) copy-start(bf16[2,16,16,16,20]{4,3,2,1,0:T(8,128)(2,1)} %concatenate.27) | copy-start | bytes 983044
  25.0 3.6 %copy-start.6 = (bf16[2,16,16,16,20]{4,3,2,1,0:T(8,128)(2,1)S(1)}, bf16[2,16,16,16,20]{4,3,2,1,0:T(8,128)(2,1)}, u32[]{:S(2)}) copy-start(bf16[2,16,16,16,20]{4,3,2,1,0:T(8,128)(2,1)} %concatenate.26) | copy-start | bytes 983044
  28.6 4.4 %copy-start.22 = (f32[1,640]{1,0:T(1,128)S(1)}, f32[1,640]{1,0:T(1,128)}, u32[]{:S(2)}) copy-start(f32[1,640]{1,0:T(1,128)} %param.23) | copy-start | bytes 7684
  28.6 5.0 %copy-start.23 = (f32[1,640]{1,0:T(1,128)S(1)}, f32[1,640]{1,0:T(1,128)}, u32[]{:S(2)}) copy-start(f32[1,640]{1,0:T(1,128)} %param.22) | copy-start | bytes 7684
  34.3 3.5 %copy-start.20 = (f32[2,32]{1,0:T(2,128)}, f32[2,32]{1,0:T(2,128)S(1)}, u32[]{:S(2)}) copy-start(f32[2,32]{1,0:T(2,128)S(1)} %broadcast_multiply_fusion.1) | copy-start | bytes 772
  49.1 2.0 %copy-start.26 = (bf16[1,3,3,640,320]{3,4,2,1,0:T(8,128)(2,1)S(1)}, bf16[1,3,3,640,320]{3,4,2,1,0:T(8,128)(2,1)}, u32[]{:S(2)}) copy-start(bf16[1,3,3,640,320]{3,4,2,1,0:T(8,128)(2,1)} %param.20) | copy-start | bytes 11059204
  49.1 2.0 %copy-start.29 = (pred[16,3]{0,1:T(4,128)(4,1)S(1)}, pred[16,3]{0,1:T(4,128)(4,1)}, u32[]{:S(2)}) copy-start(pred[16,3]{0,1:T(4,128)(4,1)} %constant.59) | copy-start | bytes 148
  56.6 17.9 %copy-start.18 = (f32[320]{0:T(512)}, f32[320]{0:T(512)S(1)}, u32[]{:S(2)}) copy-start(f32[320]{0:T(512)S(1)} %reduce.13) | copy-start | bytes 3844
  58.5 10.8 %collective-permute-start.1 = (bf16[2,16,16,320]{3,1,2,0:T(8,128)(2,1)}, bf16[2,16,16,320]{3,1,2,0:T(8,128)(2,1)S(1)}, u32[]{:S(2)}, u32[]{:S(2)}) collective-permute-start(bf16[2,16,16,320]{3,1,2,0:T(8,128)(2,1)} %fusion.73), channel_id=1, source_target_pairs={{0,16},{16,0},{1,17},{17,1},{2,18},{18,2},{3,19},{19,3},{4,20},{20... | collective-permute-start | bytes 983048 | tf_op jit(solution)/shard_map/ppermute | solution.py:19
  70.6 7.6 %copy-start.8 = (bf16[2,16,16,320]{3,1,2,0:T(8,128)(2,1)}, bf16[2,16,16,320]{3,1,2,0:T(8,128)(2,1)S(1)}, u32[]{:S(2)}) copy-start(bf16[2,16,16,320]{3,1,2,0:T(8,128)(2,1)S(1)} %get-tuple-element.10) | copy-start | bytes 983044
  78.2 3.1 %copy-start.1 = (bf16[2,16,16,16,20]{4,3,1,2,0:T(8,128)(2,1)S(1)}, bf16[2,16,16,16,20]{4,3,1,2,0:T(8,128)(2,1)}, u32[]{:S(2)}) copy-start(bf16[2,16,16,16,20]{4,3,1,2,0:T(8,128)(2,1)} %concatenate.30) | copy-start | bytes 983044
  78.2 3.5 %copy-start.3 = (bf16[2,16,16,16,20]{4,3,1,2,0:T(8,128)(2,1)S(1)}, bf16[2,16,16,16,20]{4,3,1,2,0:T(8,128)(2,1)}, u32[]{:S(2)}) copy-start(bf16[2,16,16,16,20]{4,3,1,2,0:T(8,128)(2,1)} %concatenate.29) | copy-start | bytes 983044
  81.7 3.8 %copy-start.11 = (bf16[2,16,16,320]{3,2,1,0:T(8,128)(2,1)S(1)}, bf16[2,16,16,320]{3,2,1,0:T(8,128)(2,1)}, u32[]{:S(2)}) copy-start(bf16[2,16,16,320]{3,2,1,0:T(8,128)(2,1)} %param.14) | copy-start | bytes 983044
  81.7 4.9 %copy-start.13 = (f32[320]{0:T(512)S(1)}, f32[320]{0:T(512)}, u32[]{:S(2)}) copy-start(f32[320]{0:T(512)} %copy-done.12) | copy-start | bytes 3844
  81.7 4.9 %copy-start.15 = (f32[320]{0:T(512)S(1)}, f32[320]{0:T(512)}, u32[]{:S(2)}) copy-start(f32[320]{0:T(512)} %copy-done.14) | copy-start | bytes 3844
  90.3 5.1 %copy-start.2 = (bf16[2,16,16,16,20]{4,3,1,2,0:T(8,128)(2,1)S(1)}, bf16[2,16,16,16,20]{4,3,1,2,0:T(8,128)(2,1)}, u32[]{:S(2)}) copy-start(bf16[2,16,16,16,20]{4,3,1,2,0:T(8,128)(2,1)} %concatenate.30) | copy-start | bytes 983044
  90.3 5.1 %copy-start.4 = (bf16[2,16,16,16,20]{4,3,1,2,0:T(8,128)(2,1)S(1)}, bf16[2,16,16,16,20]{4,3,1,2,0:T(8,128)(2,1)}, u32[]{:S(2)}) copy-start(bf16[2,16,16,16,20]{4,3,1,2,0:T(8,128)(2,1)} %concatenate.29) | copy-start | bytes 983044
  93.0 26.1 %collective-permute-start.2 = (bf16[2,16,16,320]{3,1,2,0:T(8,128)(2,1)}, bf16[2,16,16,320]{3,1,2,0:T(8,128)(2,1)}, u32[]{:S(2)}, u32[]{:S(2)}) collective-permute-start(bf16[2,16,16,320]{3,1,2,0:T(8,128)(2,1)} %fusion.67), channel_id=1, source_target_pairs={{0,16},{16,0},{1,17},{17,1},{2,18},{18,2},{3,19},{19,3},{4,20},{20... | collective-permute-start | bytes 983048 | tf_op jit(solution)/shard_map/ppermute | solution.py:13
  95.4 2.0 %copy-start.21 = (f32[2,32]{1,0:T(2,128)}, f32[2,32]{1,0:T(2,128)S(1)}, u32[]{:S(2)}) copy-start(f32[2,32]{1,0:T(2,128)S(1)} %broadcast_multiply_fusion) | copy-start | bytes 772
  109.0 2.0 %copy-start.27 = (bf16[1,3,3,640,320]{3,4,2,1,0:T(8,128)(2,1)S(1)}, bf16[1,3,3,640,320]{3,4,2,1,0:T(8,128)(2,1)}, u32[]{:S(2)}) copy-start(bf16[1,3,3,640,320]{3,4,2,1,0:T(8,128)(2,1)} %param.20) | copy-start | bytes 11059204
  109.0 2.0 %copy-start.30 = (pred[16,3]{0,1:T(4,128)(4,1)S(1)}, pred[16,3]{0,1:T(4,128)(4,1)}, u32[]{:S(2)}) copy-start(pred[16,3]{0,1:T(4,128)(4,1)} %constant.59) | copy-start | bytes 148
  115.8 1.0 copy-start.9
  115.8 1.0 copy-start.19
  (2 other events, 1.4 us)
where the time goes:
time: 122 us; the launch traced here: 121 us
  local copies, waits for them, and re-layouts  49.8 us (41%)
  other arithmetic  40.7 us (33%)
  matrix products  14.6 us (12%)
  waiting for transfers between devices  10.7 us (9%)
  starting transfers between devices  4.39 us (4%)
    convert_element_type x2, local copies, waits for them, and re-layouts, decode(): joined = jnp.concatenate([current, skipped], axis=3).astype(jnp.float32)  15.7 us
    concatenate x4, local copies, waits for them, and re-layouts, decode(): joined = jnp.concatenate([current, skipped], axis=3).astype(jnp.float32)  14.9 us
    conv_general_dilated x4, matrix products, convolve(): lax.conv_general_dilated(inputs, kernel, (1, 1), 'SAME', dimension_number...  14.6 us
    ppermute x2, waiting for transfers between devices, from_behind(): return lax.ppermute(value, axis, pairs)  10.7 us
    unnamed x67, local copies, waits for them, and re-layouts  8.71 us
    convert_element_type x2, other arithmetic, decode(): joined = jnp.concatenate([current, skipped], axis=3).astype(jnp.float32)  8.22 us
    reduce_sum x6, other arithmetic, norm_silu(): average = jnp.mean(grouped, axis=(1, 2, 4), keepdims=True)  8.06 us
    reduce_sum x6, other arithmetic, norm_silu(): variance = jnp.mean(centred * centred, axis=(1, 2, 4), keepdims=True)  6.93 us
  transfers between devices with their start and end apart: 3, of which 1 were waited for; matrix products, arithmetic and copies ran while one was open for 52% of the time, Pallas kernels for 0%

commit v1 on v0

v1 whole, which is shorter than its diff:
```python
import functools

import jax
import jax.numpy as jnp
from jax import lax
from jax.experimental import pallas as pl
from jax.experimental.pallas import tpu as pltpu
from jax.sharding import PartitionSpec as P

GROUPS = 32
LANES = 256
F32 = jnp.float32
BF16 = jnp.bfloat16
MESH = pl.DeviceIdType.MESH


def membership(width, per_group):
    row = lax.broadcasted_iota(jnp.int32, (width, width), 0).astype(F32)
    column = lax.broadcasted_iota(jnp.int32, (width, width), 1).astype(F32)
    same = jnp.floor((row + 0.5) * (1.0 / per_group)) == jnp.floor((column + 0.5) * (1.0 / per_group))
    return jnp.where(same, 1.0, 0.0).astype(BF16)


def group_total(values, member):
    part = jnp.sum(values.reshape(values.shape[0] // 8, 8, values.shape[1]), axis=0)
    high = part.astype(BF16).astype(F32)
    rest = part - high
    middle = rest.astype(BF16).astype(F32)
    low = rest - middle
    pieces = jnp.concatenate([high, middle, low], axis=0).astype(BF16)
    return jnp.sum(jnp.dot(pieces, member, preferred_element_type=F32), axis=0, keepdims=True)


def norm_silu(values, member, per_group, gain, beta):
    share = 1.0 / (values.shape[0] * per_group)
    centred = values - group_total(values, member) * share
    variance = group_total(centred * centred, member) * share
    half = centred * (lax.rsqrt(variance + 1e-05) * (0.5 * gain)) + 0.5 * beta
    return half + half * jnp.tanh(half)


def spread(buffer, values, side, pitch, offset):
    rows, width = values.shape
    cell = lax.rem(lax.broadcasted_iota(jnp.int32, (rows, width), 0), side)
    before = jnp.where(cell == 0, 0.0, pltpu.roll(values, 1, 0))
    after = jnp.where(cell == side - 1, 0.0, pltpu.roll(values, rows - 1, 0))
    for tap, moved in enumerate((before, values, after)):
        at = tap * pitch + offset
        buffer[side : side + rows, at : at + width] = moved.astype(BF16)


def conv_add(out, start, buffer, weight, tail, source, bias, side):
    rows, width = source.shape
    wide = width // LANES * LANES
    narrow = width - wide
    total = source[:, :wide] + bias[:, :wide]
    for tap in range(3):
        total += jnp.dot(
            buffer[tap * side : tap * side + rows, :], weight[tap, :, :wide], preferred_element_type=F32
        )
    out[start : start + rows, :wide] = total.astype(BF16)
    ends = jnp.dot(buffer[...], tail[...], preferred_element_type=F32)
    total = source[:, wide:] + bias[:, wide:]
    for tap in range(3):
        total += ends[tap * side : tap * side + rows, tap * narrow : (tap + 1) * narrow]
    out[start : start + rows, wide:] = total.astype(BF16)


def relay(sections, ticks, images, side, *refs):
    (enc_in, dec_in, fresh, queue, enc_w, enc_b, enc_g, enc_o, dec_w, dec_b, dec_g, dec_o) = refs[:12]
    (encoded, decoded, queued) = refs[12:15]
    (e0, d0, fr, sk, we, be, ge, oe, wd, bd, gd, od) = refs[15:27]
    (enc_out, dec_out, q_buf, e_buf, d_buf, enc_cols, dec_cols, enc_tail, dec_tail) = refs[27:36]
    (load_sem, store_sem, q_send, q_recv, e_send, e_recv, d_send, d_recv) = refs[36:]
    me = lax.axis_index("section")
    mirror = sections - 1 - me
    rows = side * side
    channels = e0.shape[1]

    barrier = pltpu.get_barrier_semaphore()
    pl.semaphore_signal(barrier, inc=1, device_id={"section": mirror}, device_id_type=MESH)
    if sections > 2:
        behind = jnp.logical_and(me > 0, me - 1 != mirror)
        ahead = jnp.logical_and(me < sections - 1, me + 1 != mirror)

        @pl.when(behind)
        def _():
            pl.semaphore_signal(barrier, inc=1, device_id={"section": me - 1}, device_id_type=MESH)

    loads = []
    for source, target in (
        (enc_in, e0), (enc_g, ge), (enc_o, oe), (enc_w, we), (enc_b, be), (dec_in, d0), (queue, sk),
        (dec_g, gd), (dec_o, od), (dec_w, wd), (dec_b, bd), (fresh, fr),
    ):
        copy = pltpu.make_async_copy(source, target, load_sem.at[len(loads)])
        copy.start()
        loads.append(copy)

    def span(tick, image):
        return pl.ds((tick * images + image) * rows, rows)

    def store(source, target, slot):
        return pltpu.make_async_copy(source, target, store_sem.at[slot])

    def to_mirror(tick, image):
        last = tick == ticks - 1
        return pltpu.make_async_remote_copy(
            src_ref=enc_out.at[span(tick, image)],
            dst_ref=(queued if last else q_buf).at[span(tick, image)],
            send_sem=q_send.at[tick * images + image],
            recv_sem=q_recv.at[tick * images + image],
            device_id={"section": mirror},
            device_id_type=MESH,
        )

    def to_next(source, target, send, recv, tick, image):
        return pltpu.make_async_remote_copy(
            src_ref=source.at[span(tick, image)],
            dst_ref=target.at[span(tick, image)],
            send_sem=send.at[tick * images + image],
            recv_sem=recv.at[tick * images + image],
            device_id={"section": lax.rem(me + 1, sections)},
            device_id_type=MESH,
        )

    enc_next = functools.partial(to_next, enc_out, e_buf, e_send, e_recv)
    dec_next = functools.partial(to_next, dec_out, d_buf, d_send, d_recv)

    enc_member = membership(channels, channels // GROUPS)
    dec_member = membership(channels, 2 * channels // GROUPS)
    for columns in (enc_cols, dec_cols):
        edge = jnp.zeros((images, side, columns.shape[2]), BF16)
        columns[:, :side, :] = edge
        columns[:, side + rows :, :] = edge
    wide = channels // LANES * LANES
    narrow = channels - wide
    stores = []

    for tick in range(ticks):
        for image in range(images):
            if tick == 0 and image == 0:
                for copy in loads[:3]:
                    copy.wait()
            place = span(tick, image)
            if tick == 0:
                current = e0[image * rows : (image + 1) * rows, :].astype(F32)
            else:
                if image == 0 and tick == 1:
                    loads[11].wait()
                past = span(tick - 1, image)
                to_mirror(tick - 1, image).wait_recv()
                keep = store(q_buf.at[past], queued.at[past], len(stores))
                keep.start()
                stores.append(keep)
                moved = q_buf[past, :].astype(F32)
                if sections > 2:

                    @pl.when(behind)
                    def _():
                        enc_next(tick - 1, image).wait_recv()

                    moved = jnp.where(me - 1 == mirror, moved, e_buf[past, :].astype(F32))
                current = jnp.where(me == 0, fr[past, :].astype(F32), moved)
            hidden = norm_silu(current, enc_member, channels // GROUPS, ge[...], oe[...])
            spread(enc_cols.at[image], hidden, side, channels, 0)
            if tick == 0 and image == 0:
                for copy in loads[3:5]:
                    copy.wait()
                for tap in range(3):
                    enc_tail[:, tap * narrow : (tap + 1) * narrow] = we[tap, :, wide:]
            conv_add(
                enc_out, (tick * images + image) * rows, enc_cols.at[image], we, enc_tail, current, be[...], side
            )
            if tick == 0 and image == 0:
                pl.semaphore_wait(barrier, 1)
                if sections > 2:

                    @pl.when(ahead)
                    def _():
                        pl.semaphore_wait(barrier, 1)

            to_mirror(tick, image).start()
            if sections > 2 and tick < ticks - 1:

                @pl.when(ahead)
                def _():
                    enc_next(tick, image).start()

            keep = store(enc_out.at[place], encoded.at[place], len(stores))
            keep.start()
            stores.append(keep)

        for image in range(images):
            if tick == 0 and image == 0:
                for copy in loads[5:9]:
                    copy.wait()
            place = span(tick, image)
            skipped = sk[place, :].astype(F32)
            if tick == 0:
                current = d0[image * rows : (image + 1) * rows, :].astype(F32)
            else:
                past = span(tick - 1, image)

                @pl.when(me > 0)
                def _():
                    dec_next(tick - 1, image).wait_recv()

                moved = q_buf[past, :].astype(F32)
                current = jnp.where(me == 0, moved, d_buf[past, :].astype(F32))
                skipped = jnp.where(me == 0, moved, skipped)
            for half, values in enumerate((current, skipped)):
                lanes = slice(half * channels, (half + 1) * channels)
                hidden = norm_silu(values, dec_member, 2 * channels // GROUPS, gd[:, lanes], od[:, lanes])
                spread(dec_cols.at[image], hidden, side, 2 * channels, half * channels)
            if tick == 0 and image == 0:
                for copy in loads[9:11]:
                    copy.wait()
                for tap in range(3):
                    dec_tail[:, tap * narrow : (tap + 1) * narrow] = wd[tap, :, wide:]
            conv_add(
                dec_out, (tick * images + image) * rows, dec_cols.at[image], wd, dec_tail, current, bd[...], side
            )
            if tick < ticks - 1:

                @pl.when(me < sections - 1)
                def _():
                    dec_next(tick, image).start()

            keep = store(dec_out.at[place], decoded.at[place], len(stores))
            keep.start()
            stores.append(keep)

    for keep in stores:
        keep.wait()
    for tick in range(ticks):
        for image in range(images):
            to_mirror(tick, image).wait_send()
            if tick == ticks - 1:
                to_mirror(tick, image).wait_recv()
            else:
                if sections > 2:

                    @pl.when(ahead)
                    def _():
                        enc_next(tick, image).wait_send()

                @pl.when(me < sections - 1)
                def _():
                    dec_next(tick, image).wait_send()


def shards(sections, enc_in, dec_in, fresh, skip_queue, enc_weight, enc_bias, enc_gain, enc_beta,
           dec_weight, dec_bias, dec_gain, dec_beta):
    images, side, _, channels = enc_in.shape
    ticks = skip_queue.shape[0] // images
    rows = side * side

    def flat(maps):
        return maps.reshape(maps.shape[0] * rows, channels)

    def taps(kernel):
        return kernel.reshape(3, 3 * kernel.shape[3], channels)

    operands = (
        flat(enc_in), flat(dec_in), flat(fresh), flat(skip_queue),
        taps(enc_weight), enc_bias, enc_gain, enc_beta,
        taps(dec_weight), dec_bias, dec_gain, dec_beta,
    )
    total = ticks * images * rows
    maps = jax.ShapeDtypeStruct((total, channels), BF16)
    narrow = channels % LANES
    steps = ticks * images
    anywhere = pl.BlockSpec(memory_space=pl.ANY)
    outs = pl.pallas_call(
        functools.partial(relay, sections, ticks, images, side),
        out_shape=(maps, maps, maps),
        in_specs=[anywhere] * len(operands),
        out_specs=[anywhere] * 3,
        scratch_shapes=[pltpu.VMEM(value.shape, value.dtype) for value in operands]
        + [
            pltpu.VMEM((total, channels), BF16),
            pltpu.VMEM((total, channels), BF16),
            pltpu.VMEM((total, channels), BF16),
            pltpu.VMEM((total if sections > 2 else 16, channels), BF16),
            pltpu.VMEM((total, channels), BF16),
            pltpu.VMEM((images, rows + 2 * side, 3 * channels), BF16),
            pltpu.VMEM((images, rows + 2 * side, 6 * channels), BF16),
            pltpu.VMEM((3 * channels, 3 * narrow), BF16),
            pltpu.VMEM((6 * channels, 3 * narrow), BF16),
            pltpu.SemaphoreType.DMA((len(operands),)),
            pltpu.SemaphoreType.DMA((3 * steps,)),
        ]
        + [pltpu.SemaphoreType.DMA((steps,))] * 6,
        compiler_params=pltpu.CompilerParams(
            collective_id=0, has_side_effects=True, vmem_limit_bytes=56 * 1024 * 1024
        ),
        cost_estimate=pl.CostEstimate(
            flops=steps * rows * 2 * 27 * channels * channels, bytes_accessed=12 * 1024 * 1024, transcendentals=0
        ),
    )(*operands)
    return tuple(out.reshape(ticks * images, side, side, channels) for out in outs)


def solution(mesh):
    maps = P(("dp", "section"), None, None, None)
    row = P("section", None)
    kernel = P("section", None, None, None, None)
    in_specs = (maps, maps, P("dp", None, None, None), maps, kernel, row, row, row, kernel, row, row, row)
    return jax.shard_map(
        functools.partial(shards, mesh.shape["section"]),
        mesh=mesh,
        in_specs=in_specs,
        out_specs=(maps, maps, maps),
        check_vma=False,
    )
```

time: 122 us -> 43.7 us (0.36)
  the two profiles are of different devices: /device:TPU:0 before, /device:TPU:10 now
where the time goes in v1:
time: 43.7 us; the launch traced here: 43.3 us
  Pallas kernels  29.8 us (68%)
  local copies, waits for them, and re-layouts  12.9 us (30%)
  between operations  0.65 us (1%)
    pallas_call x1, Pallas kernels, shards(): pl.pallas_call(functools.partial(relay, sections, ticks, images, side), o...  29.8 us
    unnamed x6, local copies, waits for them, and re-layouts  12.9 us

profile of v1, /device:TPU:10, one launch (start us, length us, event | category | flops | bytes accessed | tf_op | source)
XLA Modules:
  0.0 43.3 jit_solution(16980973281527715033)
XLA Ops:
  0.6 7.8 %copy.15 = bf16[1,3,3,640,320]{4,3,2,1,0:T(8,128)(2,1)} copy(bf16[1,3,3,640,320]{3,4,2,1,0:T(8,128)(2,1)} %param.20) | data formatting | bytes 7372800 | tf_op args[8]
  8.4 29.8 %shard_map.139 = (bf16[1024,320]{1,0:T(8,128)(2,1)}, bf16[1024,320]{1,0:T(8,128)(2,1)}, bf16[1024,320]{1,0:T(8,128)(2,1)}) custom-call(bf16[512,320]{1,0:T(8,128)(2,1)} %bitcast.15, bf16[512,320]{1,0:T(8,128)(2,1)} %bitcast.16, bf16[512,320]{1,0:T(8,128)(2,1)} %bitcast.17, bf16[1024,320]{1,0:T(8,128)(2,1)} %bitcast.14, bf16[3,960,320]{2,1,0:T(8,128)(2,1)} %bitcast.13, ...), custom_call_target="tpu_custom_call" | custom-call | flops 5662310400 | bytes 12582912 | tf_op jit(solution)/shard_map/pallas_call | solution.py:274
  38.2 0.0 copy-start
  38.2 2.2 %copy.19 = bf16[4,16,16,320]{3,2,1,0:T(8,128)(2,1)} copy(bf16[4,16,16,320]{3,2,1,0:T(8,128)(2,1)} %bitcast.12) | data formatting | bytes 1310720
  40.3 2.1 %copy.20 = bf16[4,16,16,320]{3,2,1,0:T(8,128)(2,1)} copy(bf16[4,16,16,320]{3,2,1,0:T(8,128)(2,1)} %bitcast.11) | data formatting | bytes 1310720
  42.4 0.0 copy-done
  42.4 0.9 %copy.21 = bf16[4,16,16,320]{3,2,1,0:T(8,128)(2,1)} copy(bf16[4,16,16,320]{3,2,1,0:T(8,128)(2,1)S(1)} %bitcast.10) | data formatting | bytes 1310720
Async XLA Ops:
  38.2 4.3 %copy-start = (bf16[1024,320]{1,0:T(8,128)(2,1)S(1)}, bf16[1024,320]{1,0:T(8,128)(2,1)}, u32[]{:S(2)}) copy-start(bf16[1024,320]{1,0:T(8,128)(2,1)} %get-tuple-element.8) | copy-start | bytes 1966084

commit v2 on v1

--- a/solution.py
+++ b/solution.py
@@ -49,33 +49,64 @@
         buffer[side : side + rows, at : at + width] = moved.astype(BF16)
 
 
-def conv_add(out, start, buffer, weight, tail, source, bias, side):
+def product(left, right, flipped):
+    return lax.dot_general(left, right, (((1,), (1 if flipped else 0,)), ((), ())), preferred_element_type=F32)
+
+
+def pack(target, start, wide, tail):
+    rows, narrow = tail.shape
+    depth = rows * narrow // wide.shape[1]
+    target[start : start + rows, :] = wide
+    for part in range(rows // depth):
+        target[start + rows : start + rows + depth, part * narrow : (part + 1) * narrow] = tail[
+            part * depth : (part + 1) * depth, :
+        ]
+
+
+def unpack(source, start, rows, narrow):
+    depth = rows * narrow // source.shape[1]
+    tail = [
+        source[start + rows : start + rows + depth, part * narrow : (part + 1) * narrow]
+        for part in range(rows // depth)
+    ]
+    return source[start : start + rows, :], jnp.concatenate(tail, axis=0)
+
+
+def conv_add(out, packed, step, buffer, weight, tail, flipped, source, bias, side):
     rows, width = source.shape
+    start = step * rows
     wide = width // LANES * LANES
     narrow = width - wide
     total = source[:, :wide] + bias[:, :wide]
     for tap in range(3):
-        total += jnp.dot(
-            buffer[tap * side : tap * side + rows, :], weight[tap, :, :wide], preferred_element_type=F32
+        total += product(
+            buffer[tap * side : tap * side + rows, :], weight[tap] if flipped else weight[tap, :, :wide], flipped
         )
-    out[start : start + rows, :wide] = total.astype(BF16)
-    ends = jnp.dot(buffer[...], tail[...], preferred_element_type=F32)
+    main = total.astype(BF16)
+    out[start : start + rows, :wide] = main
+    ends = product(buffer[...], tail[...], flipped)
     total = source[:, wide:] + bias[:, wide:]
     for tap in range(3):
         total += ends[tap * side : tap * side + rows, tap * narrow : (tap + 1) * narrow]
-    out[start : start + rows, wide:] = total.astype(BF16)
+    rest = total.astype(BF16)
+    out[start : start + rows, wide:] = rest
+    pack(packed, step * packed.shape[0] // (out.shape[0] // rows), main, rest)
 
 
 def relay(sections, ticks, images, side, *refs):
     (enc_in, dec_in, fresh, queue, enc_w, enc_b, enc_g, enc_o, dec_w, dec_b, dec_g, dec_o) = refs[:12]
     (encoded, decoded, queued) = refs[12:15]
     (e0, d0, fr, sk, we, be, ge, oe, wd, bd, gd, od) = refs[15:27]
-    (enc_out, dec_out, q_buf, e_buf, d_buf, enc_cols, dec_cols, enc_tail, dec_tail) = refs[27:36]
-    (load_sem, store_sem, q_send, q_recv, e_send, e_recv, d_send, d_recv) = refs[36:]
+    (enc_out, dec_out, q_out, enc_pack, dec_pack, q_buf, e_buf, d_buf) = refs[27:35]
+    (enc_cols, dec_cols, enc_tail, dec_tail) = refs[35:39]
+    (load_sem, store_sem, q_send, q_recv, e_send, e_recv, d_send, d_recv) = refs[39:]
     me = lax.axis_index("section")
     mirror = sections - 1 - me
     rows = side * side
     channels = e0.shape[1]
+    wide = channels // LANES * LANES
+    narrow = channels - wide
+    packed = rows * channels // wide
 
     barrier = pltpu.get_barrier_semaphore()
     pl.semaphore_signal(barrier, inc=1, device_id={"section": mirror}, device_id_type=MESH)
@@ -88,10 +119,16 @@
             pl.semaphore_signal(barrier, inc=1, device_id={"section": me - 1}, device_id_type=MESH)
 
     loads = []
-    for source, target in (
+    moves = [
         (enc_in, e0), (enc_g, ge), (enc_o, oe), (enc_w, we), (enc_b, be), (dec_in, d0), (queue, sk),
-        (dec_g, gd), (dec_o, od), (dec_w, wd), (dec_b, bd), (fresh, fr),
-    ):
+        (dec_g, gd), (dec_o, od), (dec_b, bd), (fresh, fr),
+    ]
+    for tap in range(9):
+        lanes = pl.ds(tap % 3 * 2 * channels, 2 * channels)
+        source = dec_w.at[tap]
+        moves.append((source.at[pl.ds(0, wide)], wd.at[tap // 3, :, lanes]))
+        moves.append((source.at[pl.ds(wide, narrow)], dec_tail.at[pl.ds(tap // 3 * narrow, narrow), lanes]))
+    for source, target in moves:
         copy = pltpu.make_async_copy(source, target, load_sem.at[len(loads)])
         copy.start()
         loads.append(copy)
@@ -102,11 +139,28 @@
     def store(source, target, slot):
         return pltpu.make_async_copy(source, target, store_sem.at[slot])
 
+    def bundle(tick, image):
+        return pl.ds((tick * images + image) * packed, packed)
+
+    def opened(source, tick, image):
+        return unpack(source, (tick * images + image) * packed, rows, narrow)
+
+    def joined(source, tick, image):
+        return jnp.concatenate([part.astype(F32) for part in opened(source, tick, image)], axis=1)
+
+    def keep_mirrored(tick, image):
+        main, rest = opened(q_buf, tick, image)
+        start = (tick * images + image) * rows
+        q_out[start : start + rows, :wide] = main
+        q_out[start : start + rows, wide:] = rest
+        keep = store(q_out.at[span(tick, image)], queued.at[span(tick, image)], len(stores))
+        keep.start()
+        stores.append(keep)
+
     def to_mirror(tick, image):
-        last = tick == ticks - 1
         return pltpu.make_async_remote_copy(
-            src_ref=enc_out.at[span(tick, image)],
-            dst_ref=(queued if last else q_buf).at[span(tick, image)],
+            src_ref=enc_pack.at[bundle(tick, image)],
+            dst_ref=q_buf.at[bundle(tick, image)],
             send_sem=q_send.at[tick * images + image],
             recv_sem=q_recv.at[tick * images + image],
             device_id={"section": mirror},
@@ -115,16 +169,16 @@
 
     def to_next(source, target, send, recv, tick, image):
         return pltpu.make_async_remote_copy(
-            src_ref=source.at[span(tick, image)],
-            dst_ref=target.at[span(tick, image)],
+            src_ref=source.at[bundle(tick, image)],
+            dst_ref=target.at[bundle(tick, image)],
             send_sem=send.at[tick * images + image],
             recv_sem=recv.at[tick * images + image],
             device_id={"section": lax.rem(me + 1, sections)},
             device_id_type=MESH,
         )
 
-    enc_next = functools.partial(to_next, enc_out, e_buf, e_send, e_recv)
-    dec_next = functools.partial(to_next, dec_out, d_buf, d_send, d_recv)
+    enc_next = functools.partial(to_next, enc_pack, e_buf, e_send, e_recv)
+    dec_next = functools.partial(to_next, dec_pack, d_buf, d_send, d_recv)
 
     enc_member = membership(channels, channels // GROUPS)
     dec_member = membership(channels, 2 * channels // GROUPS)
@@ -132,8 +186,6 @@
         edge = jnp.zeros((images, side, columns.shape[2]), BF16)
         columns[:, :side, :] = edge
         columns[:, side + rows :, :] = edge
-    wide = channels // LANES * LANES
-    narrow = channels - wide
     stores = []
 
     for tick in range(ticks):
@@ -146,20 +198,18 @@
                 current = e0[image * rows : (image + 1) * rows, :].astype(F32)
             else:
                 if image == 0 and tick == 1:
-                    loads[11].wait()
+                    loads[10].wait()
                 past = span(tick - 1, image)
                 to_mirror(tick - 1, image).wait_recv()
-                keep = store(q_buf.at[past], queued.at[past], len(stores))
-                keep.start()
-                stores.append(keep)
-                moved = q_buf[past, :].astype(F32)
+                keep_mirrored(tick - 1, image)
+                moved = joined(q_buf, tick - 1, image)
                 if sections > 2:
 
                     @pl.when(behind)
                     def _():
                         enc_next(tick - 1, image).wait_recv()
 
-                    moved = jnp.where(me - 1 == mirror, moved, e_buf[past, :].astype(F32))
+                    moved = jnp.where(me - 1 == mirror, moved, joined(e_buf, tick - 1, image))
                 current = jnp.where(me == 0, fr[past, :].astype(F32), moved)
             hidden = norm_silu(current, enc_member, channels // GROUPS, ge[...], oe[...])
             spread(enc_cols.at[image], hidden, side, channels, 0)
@@ -169,7 +219,8 @@
                 for tap in range(3):
                     enc_tail[:, tap * narrow : (tap + 1) * narrow] = we[tap, :, wide:]
             conv_add(
-                enc_out, (tick * images + image) * rows, enc_cols.at[image], we, enc_tail, current, be[...], side
+                enc_out, enc_pack, tick * images + image, enc_cols.at[image], we, enc_tail, False, current, be[...],
+                side,
             )
             if tick == 0 and image == 0:
                 pl.semaphore_wait(barrier, 1)
@@ -199,26 +250,24 @@
             if tick == 0:
                 current = d0[image * rows : (image + 1) * rows, :].astype(F32)
             else:
-                past = span(tick - 1, image)
 
                 @pl.when(me > 0)
                 def _():
                     dec_next(tick - 1, image).wait_recv()
 
-                moved = q_buf[past, :].astype(F32)
-                current = jnp.where(me == 0, moved, d_buf[past, :].astype(F32))
+                moved = joined(q_buf, tick - 1, image)
+                current = jnp.where(me == 0, moved, joined(d_buf, tick - 1, image))
                 skipped = jnp.where(me == 0, moved, skipped)
             for half, values in enumerate((current, skipped)):
                 lanes = slice(half * channels, (half + 1) * channels)
                 hidden = norm_silu(values, dec_member, 2 * channels // GROUPS, gd[:, lanes], od[:, lanes])
                 spread(dec_cols.at[image], hidden, side, 2 * channels, half * channels)
             if tick == 0 and image == 0:
-                for copy in loads[9:11]:
+                for copy in loads[9:10] + loads[11:]:
                     copy.wait()
-                for tap in range(3):
-                    dec_tail[:, tap * narrow : (tap + 1) * narrow] = wd[tap, :, wide:]
             conv_add(
-                dec_out, (tick * images + image) * rows, dec_cols.at[image], wd, dec_tail, current, bd[...], side
+                dec_out, dec_pack, tick * images + image, dec_cols.at[image], wd, dec_tail, True, current, bd[...],
+                side,
             )
             if tick < ticks - 1:
 
@@ -230,14 +279,15 @@
             keep.start()
             stores.append(keep)
 
+    for image in range(images):
+        to_mirror(ticks - 1, image).wait_recv()
+        keep_mirrored(ticks - 1, image)
     for keep in stores:
         keep.wait()
     for tick in range(ticks):
         for image in range(images):
             to_mirror(tick, image).wait_send()
-            if tick == ticks - 1:
-                to_mirror(tick, image).wait_recv()
-            else:
+            if tick < ticks - 1:
                 if sections > 2:
 
                     @pl.when(ahead)
@@ -247,6 +297,20 @@
                 @pl.when(me < sections - 1)
                 def _():
                     dec_next(tick, image).wait_send()
+
+
+def hand_on(*refs):
+    count = len(refs) // 2
+    copies = []
+    for source, target in zip(refs[:count], refs[count:-1]):
+        half = source.shape[0] // 2
+        for part in range(2):
+            at = pl.ds(part * half, half)
+            copies.append(pltpu.make_async_copy(source.at[at], target.at[at], refs[-1].at[len(copies)]))
+    for copy in copies:
+        copy.start()
+    for copy in copies:
+        copy.wait()
 
 
 def shards(sections, enc_in, dec_in, fresh, skip_queue, enc_weight, enc_bias, enc_gain, enc_beta,
@@ -259,35 +323,43 @@
         return maps.reshape(maps.shape[0] * rows, channels)
 
     def taps(kernel):
-        return kernel.reshape(3, 3 * kernel.shape[3], channels)
+        return kernel.reshape(3, 3 * channels, channels)
 
     operands = (
         flat(enc_in), flat(dec_in), flat(fresh), flat(skip_queue),
         taps(enc_weight), enc_bias, enc_gain, enc_beta,
-        taps(dec_weight), dec_bias, dec_gain, dec_beta,
+        lax.transpose(dec_weight, (0, 1, 2, 4, 3)).reshape(9, channels, 2 * channels), dec_bias, dec_gain, dec_beta,
     )
     total = ticks * images * rows
     maps = jax.ShapeDtypeStruct((total, channels), BF16)
     narrow = channels % LANES
+    wide = channels - narrow
+    packed = pltpu.VMEM((ticks * images * rows * channels // wide, wide), BF16)
+    spare = packed if sections > 2 else pltpu.VMEM((16, wide), BF16)
+    held = [pltpu.VMEM(value.shape, value.dtype) for value in operands]
+    held[8] = pltpu.VMEM((3, wide, 6 * channels), BF16)
     steps = ticks * images
     anywhere = pl.BlockSpec(memory_space=pl.ANY)
     outs = pl.pallas_call(
         functools.partial(relay, sections, ticks, images, side),
-        out_shape=(maps, maps, maps),
+        out_shape=(pltpu.VMEM(maps.shape, maps.dtype),) * 3,
         in_specs=[anywhere] * len(operands),
         out_specs=[anywhere] * 3,
-        scratch_shapes=[pltpu.VMEM(value.shape, value.dtype) for value in operands]
+        scratch_shapes=held
         + [
             pltpu.VMEM((total, channels), BF16),
             pltpu.VMEM((total, channels), BF16),
             pltpu.VMEM((total, channels), BF16),
-            pltpu.VMEM((total if sections > 2 else 16, channels), BF16),
-            pltpu.VMEM((total, channels), BF16),
+            packed,
+            packed,
+            packed,
+            spare,
+            packed,
             pltpu.VMEM((images, rows + 2 * side, 3 * channels), BF16),
             pltpu.VMEM((images, rows + 2 * side, 6 * channels), BF16),
             pltpu.VMEM((3 * channels, 3 * narrow), BF16),
-            pltpu.VMEM((6 * channels, 3 * narrow), BF16),
-            pltpu.SemaphoreType.DMA((len(operands),)),
+            pltpu.VMEM((3 * narrow, 6 * channels), BF16),
+            pltpu.SemaphoreType.DMA((len(operands) + 17,)),
             pltpu.SemaphoreType.DMA((3 * steps,)),
         ]
         + [pltpu.SemaphoreType.DMA((steps,))] * 6,
@@ -298,6 +370,13 @@
             flops=steps * rows * 2 * 27 * channels * channels, bytes_accessed=12 * 1024 * 1024, transcendentals=0
         ),
     )(*operands)
+    outs = pl.pallas_call(
+        hand_on,
+        out_shape=(maps, maps, maps),
+        in_specs=[anywhere] * 3,
+        out_specs=[anywhere] * 3,
+        scratch_shapes=[pltpu.SemaphoreType.DMA((6,))],
+    )(*outs)
     return tuple(out.reshape(ticks * images, side, side, channels) for out in outs)
 
 

time: 43.7 us -> 102 us (2.33)
  Pallas kernels: 29.8 us -> 99 us
  local copies, waits for them, and re-layouts: 12.9 us -> 2.68 us
    pallas_call x0 -> x1, Pallas kernels: none -> 72.6 us  [shards(): pl.pallas_call(hand_on, out_shape=(maps, maps, maps), in_specs=[anywhere]...]
    unnamed x6, local copies, waits for them, and re-layouts: 12.9 us -> 2.68 us
    pallas_call x1, Pallas kernels: 29.8 us -> 26.3 us  [shards(): pl.pallas_call(functools.partial(relay, sections, ticks, images, side), o...]
where the time goes in v2:
time: 102 us
  Pallas kernels  99 us (97%)
  local copies, waits for them, and re-layouts  2.68 us (3%)
    pallas_call x1, Pallas kernels, shards(): pl.pallas_call(hand_on, out_shape=(maps, maps, maps), in_specs=[anywhere]...  72.6 us
    pallas_call x1, Pallas kernels, shards(): pl.pallas_call(functools.partial(relay, sections, ticks, images, side), o...  26.3 us
    unnamed x6, local copies, waits for them, and re-layouts  2.68 us

profile of v2, /device:TPU:10, one launch (start us, length us, event | category | flops | bytes accessed | tf_op | source)
XLA Modules:
  0.0 102.3 jit_solution(1389251237221471328)
XLA Ops:
  0.6 26.3 %shard_map.139 = (bf16[1024,320]{1,0:T(8,128)(2,1)S(1)}, bf16[1024,320]{1,0:T(8,128)(2,1)S(1)}, bf16[1024,320]{1,0:T(8,128)(2,1)S(1)}) custom-call(bf16[512,320]{1,0:T(8,128)(2,1)} %bitcast.17, bf16[512,320]{1,0:T(8,128)(2,1)} %bitcast.18, bf16[512,320]{1,0:T(8,128)(2,1)} %bitcast.19, bf16[1024,320]{1,0:T(8,128)(2,1)} %bitcast.13, ...), custom_call_target="tpu_custom_call" | custom-call | flops 5662310400 | bytes 12582912 | tf_op jit(solution)/shard_map/pallas_call | solution.py:343
  27.0 0.0 copy-start
  27.0 0.9 copy-done
  27.9 0.0 copy-start.1
  27.9 0.9 copy-done.1
  28.8 0.0 copy-start.2
  28.8 0.9 copy-done.2
  29.7 72.6 %shard_map.140 = (bf16[1024,320]{1,0:T(8,128)(2,1)}, bf16[1024,320]{1,0:T(8,128)(2,1)}, bf16[1024,320]{1,0:T(8,128)(2,1)}) custom-call(bf16[1024,320]{1,0:T(8,128)(2,1)} %copy-done, bf16[1024,320]{1,0:T(8,128)(2,1)} %copy-done.1, bf16[1024,320]{1,0:T(8,128)(2,1)} %copy-done.2), custom_call_target="tpu_custom_call" | custom-call | tf_op jit(solution)/shard_map/pallas_call | solution.py:373
Async XLA Ops:
  27.0 0.9 copy-start
  27.9 0.9 copy-start.1
  28.8 0.9 copy-start.2

commit v3 on v2

--- a/solution.py
+++ b/solution.py
@@ -97,9 +97,8 @@
     (enc_in, dec_in, fresh, queue, enc_w, enc_b, enc_g, enc_o, dec_w, dec_b, dec_g, dec_o) = refs[:12]
     (encoded, decoded, queued) = refs[12:15]
     (e0, d0, fr, sk, we, be, ge, oe, wd, bd, gd, od) = refs[15:27]
-    (enc_out, dec_out, q_out, enc_pack, dec_pack, q_buf, e_buf, d_buf) = refs[27:35]
-    (enc_cols, dec_cols, enc_tail, dec_tail) = refs[35:39]
-    (load_sem, store_sem, q_send, q_recv, e_send, e_recv, d_send, d_recv) = refs[39:]
+    (enc_pack, dec_pack, q_buf, e_buf, d_buf, enc_cols, dec_cols, enc_tail, dec_tail) = refs[27:36]
+    (load_sem, q_send, q_recv, e_send, e_recv, d_send, d_recv) = refs[36:]
     me = lax.axis_index("section")
     mirror = sections - 1 - me
     rows = side * side
@@ -130,14 +129,12 @@
         moves.append((source.at[pl.ds(wide, narrow)], dec_tail.at[pl.ds(tap // 3 * narrow, narrow), lanes]))
     for source, target in moves:
         copy = pltpu.make_async_copy(source, target, load_sem.at[len(loads)])
+        loads.append(copy)
+    for copy in loads[:5]:
         copy.start()
-        loads.append(copy)
 
     def span(tick, image):
         return pl.ds((tick * images + image) * rows, rows)
-
-    def store(source, target, slot):
-        return pltpu.make_async_copy(source, target, store_sem.at[slot])
 
     def bundle(tick, image):
         return pl.ds((tick * images + image) * packed, packed)
@@ -151,11 +148,8 @@
     def keep_mirrored(tick, image):
         main, rest = opened(q_buf, tick, image)
         start = (tick * images + image) * rows
-        q_out[start : start + rows, :wide] = main
-        q_out[start : start + rows, wide:] = rest
-        keep = store(q_out.at[span(tick, image)], queued.at[span(tick, image)], len(stores))
-        keep.start()
-        stores.append(keep)
+        queued[start : start + rows, :wide] = main
+        queued[start : start + rows, wide:] = rest
 
     def to_mirror(tick, image):
         return pltpu.make_async_remote_copy(
@@ -186,7 +180,6 @@
         edge = jnp.zeros((images, side, columns.shape[2]), BF16)
         columns[:, :side, :] = edge
         columns[:, side + rows :, :] = edge
-    stores = []
 
     for tick in range(ticks):
         for image in range(images):
@@ -216,10 +209,12 @@
             if tick == 0 and image == 0:
                 for copy in loads[3:5]:
                     copy.wait()
+                for copy in loads[5:]:
+                    copy.start()
                 for tap in range(3):
                     enc_tail[:, tap * narrow : (tap + 1) * narrow] = we[tap, :, wide:]
             conv_add(
-                enc_out, enc_pack, tick * images + image, enc_cols.at[image], we, enc_tail, False, current, be[...],
+                encoded, enc_pack, tick * images + image, enc_cols.at[image], we, enc_tail, False, current, be[...],
                 side,
             )
             if tick == 0 and image == 0:
@@ -236,10 +231,6 @@
                 @pl.when(ahead)
                 def _():
                     enc_next(tick, image).start()
-
-            keep = store(enc_out.at[place], encoded.at[place], len(stores))
-            keep.start()
-            stores.append(keep)
 
         for image in range(images):
             if tick == 0 and image == 0:
@@ -266,7 +257,7 @@
                 for copy in loads[9:10] + loads[11:]:
                     copy.wait()
             conv_add(
-                dec_out, dec_pack, tick * images + image, dec_cols.at[image], wd, dec_tail, True, current, bd[...],
+                decoded, dec_pack, tick * images + image, dec_cols.at[image], wd, dec_tail, True, current, bd[...],
                 side,
             )
             if tick < ticks - 1:
@@ -275,15 +266,9 @@
                 def _():
                     dec_next(tick, image).start()
 
-            keep = store(dec_out.at[place], decoded.at[place], len(stores))
-            keep.start()
-            stores.append(keep)
-
     for image in range(images):
         to_mirror(ticks - 1, image).wait_recv()
         keep_mirrored(ticks - 1, image)
-    for keep in stores:
-        keep.wait()
     for tick in range(ticks):
         for image in range(images):
             to_mirror(tick, image).wait_send()
@@ -344,12 +329,9 @@
         functools.partial(relay, sections, ticks, images, side),
         out_shape=(pltpu.VMEM(maps.shape, maps.dtype),) * 3,
         in_specs=[anywhere] * len(operands),
-        out_specs=[anywhere] * 3,
+        out_specs=[pl.BlockSpec(memory_space=pltpu.VMEM)] * 3,
         scratch_shapes=held
         + [
-            pltpu.VMEM((total, channels), BF16),
-            pltpu.VMEM((total, channels), BF16),
-            pltpu.VMEM((total, channels), BF16),
             packed,
             packed,
             packed,
@@ -360,7 +342,6 @@
             pltpu.VMEM((3 * channels, 3 * narrow), BF16),
             pltpu.VMEM((3 * narrow, 6 * channels), BF16),
             pltpu.SemaphoreType.DMA((len(operands) + 17,)),
-            pltpu.SemaphoreType.DMA((3 * steps,)),
         ]
         + [pltpu.SemaphoreType.DMA((steps,))] * 6,
         compiler_params=pltpu.CompilerParams(
@@ -376,6 +357,7 @@
         in_specs=[anywhere] * 3,
         out_specs=[anywhere] * 3,
         scratch_shapes=[pltpu.SemaphoreType.DMA((6,))],
+        compiler_params=pltpu.CompilerParams(vmem_limit_bytes=4 * 1024 * 1024),
     )(*outs)
     return tuple(out.reshape(ticks * images, side, side, channels) for out in outs)
 

time: 102 us -> 28.2 us (0.28)
  Pallas kernels: 99 us -> 27.4 us
  local copies, waits for them, and re-layouts: 2.68 us -> 0 us
    pallas_call x1, Pallas kernels: 72.6 us -> 1.45 us  [shards(): pl.pallas_call(hand_on, out_shape=(maps, maps, maps), in_specs=[anywhere]...]
    unnamed x6 -> x0, local copies, waits for them, and re-layouts: 2.68 us -> none
where the time goes in v3:
time: 28.2 us; the launch traced here: 28 us
  Pallas kernels  27.4 us (97%)
  between operations  0.64 us (2%)
    pallas_call x1, Pallas kernels, shards(): pl.pallas_call(functools.partial(relay, sections, ticks, images, side), o...  25.9 us
    pallas_call x1, Pallas kernels, shards(): pl.pallas_call(hand_on, out_shape=(maps, maps, maps), in_specs=[anywhere]...  1.45 us

profile of v3, /device:TPU:10, one launch (start us, length us, event | category | flops | bytes accessed | tf_op | source)
XLA Modules:
  0.0 28.0 jit_solution(2034636387522538731)
XLA Ops:
  0.6 25.9 %shard_map.139 = (bf16[1024,320]{1,0:T(8,128)(2,1)S(1)}, bf16[1024,320]{1,0:T(8,128)(2,1)S(1)}, bf16[1024,320]{1,0:T(8,128)(2,1)S(1)}) custom-call(bf16[512,320]{1,0:T(8,128)(2,1)} %bitcast.17, bf16[512,320]{1,0:T(8,128)(2,1)} %bitcast.18, bf16[512,320]{1,0:T(8,128)(2,1)} %bitcast.19, bf16[1024,320]{1,0:T(8,128)(2,1)} %bitcast.13, ...), custom_call_target="tpu_custom_call" | custom-call | flops 5662310400 | bytes 12582912 | tf_op jit(solution)/shard_map/pallas_call | solution.py:328
  26.6 1.4 %shard_map.140 = (bf16[1024,320]{1,0:T(8,128)(2,1)}, bf16[1024,320]{1,0:T(8,128)(2,1)}, bf16[1024,320]{1,0:T(8,128)(2,1)}) custom-call(bf16[1024,320]{1,0:T(8,128)(2,1)S(1)} %get-tuple-element.9.refs_0_, bf16[1024,320]{1,0:T(8,128)(2,1)S(1)} %get-tuple-element.10.refs_1_, bf16[1024,320]{1,0:T(8,128)(2,1)S(1)} %get-tuple-element.11.refs_2_), custom_call_target="tpu_custom_call" | custom-call | tf_op jit(solution)/shard_map/pallas_call | solution.py:354

commit v4 on v3

--- a/solution.py
+++ b/solution.py
@@ -31,22 +31,33 @@
     return jnp.sum(jnp.dot(pieces, member, preferred_element_type=F32), axis=0, keepdims=True)
 
 
-def norm_silu(values, member, per_group, gain, beta):
+def prepare(values, member, per_group, gain, beta, buffer, side, pitch, offset):
     share = 1.0 / (values.shape[0] * per_group)
     centred = values - group_total(values, member) * share
+    yield
     variance = group_total(centred * centred, member) * share
+    yield
     half = centred * (lax.rsqrt(variance + 1e-05) * (0.5 * gain)) + 0.5 * beta
-    return half + half * jnp.tanh(half)
-
-
-def spread(buffer, values, side, pitch, offset):
-    rows, width = values.shape
+    hidden = half + half * jnp.tanh(half)
+    rows, width = hidden.shape
     cell = lax.rem(lax.broadcasted_iota(jnp.int32, (rows, width), 0), side)
-    before = jnp.where(cell == 0, 0.0, pltpu.roll(values, 1, 0))
-    after = jnp.where(cell == side - 1, 0.0, pltpu.roll(values, rows - 1, 0))
-    for tap, moved in enumerate((before, values, after)):
-        at = tap * pitch + offset
-        buffer[side : side + rows, at : at + width] = moved.astype(BF16)
+    buffer[side : side + rows, pitch + offset : pitch + offset + width] = hidden.astype(BF16)
+    yield
+    before = jnp.where(cell == 0, 0.0, pltpu.roll(hidden, 1, 0))
+    buffer[side : side + rows, offset : offset + width] = before.astype(BF16)
+    yield
+    after = jnp.where(cell == side - 1, 0.0, pltpu.roll(hidden, rows - 1, 0))
+    buffer[side : side + rows, 2 * pitch + offset : 2 * pitch + offset + width] = after.astype(BF16)
+
+
+def weave(*works):
+    works = list(works)
+    while works:
+        for work in tuple(works):
+            try:
+                next(work)
+            except StopIteration:
+                works.remove(work)
 
 
 def product(left, right, flipped):
@@ -82,9 +93,11 @@
         total += product(
             buffer[tap * side : tap * side + rows, :], weight[tap] if flipped else weight[tap, :, :wide], flipped
         )
+        yield
     main = total.astype(BF16)
     out[start : start + rows, :wide] = main
     ends = product(buffer[...], tail[...], flipped)
+    yield
     total = source[:, wide:] + bias[:, wide:]
     for tap in range(3):
         total += ends[tap * side : tap * side + rows, tap * narrow : (tap + 1) * narrow]
@@ -174,49 +187,88 @@
     enc_next = functools.partial(to_next, enc_pack, e_buf, e_send, e_recv)
     dec_next = functools.partial(to_next, dec_pack, d_buf, d_send, d_recv)
 
-    enc_member = membership(channels, channels // GROUPS)
-    dec_member = membership(channels, 2 * channels // GROUPS)
-    for columns in (enc_cols, dec_cols):
+    def clear(columns):
         edge = jnp.zeros((images, side, columns.shape[2]), BF16)
         columns[:, :side, :] = edge
         columns[:, side + rows :, :] = edge
 
-    for tick in range(ticks):
-        for image in range(images):
-            if tick == 0 and image == 0:
-                for copy in loads[:3]:
+    def enc_source(tick, image):
+        if tick == 0:
+            return e0[image * rows : (image + 1) * rows, :].astype(F32)
+        moved = joined(q_buf, tick - 1, image)
+        if sections > 2:
+            moved = jnp.where(me - 1 == mirror, moved, joined(e_buf, tick - 1, image))
+        return jnp.where(me == 0, fr[span(tick - 1, image), :].astype(F32), moved)
+
+    def dec_source(tick, image):
+        if tick == 0:
+            return d0[image * rows : (image + 1) * rows, :].astype(F32)
+        return jnp.where(me == 0, joined(q_buf, tick - 1, image), joined(d_buf, tick - 1, image))
+
+    def dec_skip(tick, image):
+        skipped = sk[span(tick, image), :].astype(F32)
+        return skipped if tick == 0 else jnp.where(me == 0, joined(q_buf, tick - 1, image), skipped)
+
+    def arrive(is_enc, tick, image):
+        if tick == 0:
+            if image == 0 and not is_enc:
+                for copy in loads[5:9]:
                     copy.wait()
-            place = span(tick, image)
-            if tick == 0:
-                current = e0[image * rows : (image + 1) * rows, :].astype(F32)
-            else:
-                if image == 0 and tick == 1:
-                    loads[10].wait()
-                past = span(tick - 1, image)
-                to_mirror(tick - 1, image).wait_recv()
+            return
+        if is_enc:
+            if tick == 1 and image == 0:
+                loads[10].wait()
+            to_mirror(tick - 1, image).wait_recv()
+            if sections > 2:
+
+                @pl.when(behind)
+                def _():
+                    enc_next(tick - 1, image).wait_recv()
+
+            return
+
+        @pl.when(me > 0)
+        def _():
+            dec_next(tick - 1, image).wait_recv()
+
+    def ready(is_enc, tick, image):
+        if is_enc:
+            if tick > 0:
                 keep_mirrored(tick - 1, image)
-                moved = joined(q_buf, tick - 1, image)
-                if sections > 2:
-
-                    @pl.when(behind)
-                    def _():
-                        enc_next(tick - 1, image).wait_recv()
-
-                    moved = jnp.where(me - 1 == mirror, moved, joined(e_buf, tick - 1, image))
-                current = jnp.where(me == 0, fr[past, :].astype(F32), moved)
-            hidden = norm_silu(current, enc_member, channels // GROUPS, ge[...], oe[...])
-            spread(enc_cols.at[image], hidden, side, channels, 0)
-            if tick == 0 and image == 0:
-                for copy in loads[3:5]:
-                    copy.wait()
-                for copy in loads[5:]:
-                    copy.start()
-                for tap in range(3):
-                    enc_tail[:, tap * narrow : (tap + 1) * narrow] = we[tap, :, wide:]
-            conv_add(
-                encoded, enc_pack, tick * images + image, enc_cols.at[image], we, enc_tail, False, current, be[...],
-                side,
+            yield from prepare(
+                enc_source(tick, image), enc_member, channels // GROUPS, ge[...], oe[...], enc_cols.at[image],
+                side, channels, 0,
             )
+            return
+        parts = []
+        for half, values in enumerate((dec_source(tick, image), dec_skip(tick, image))):
+            lanes = slice(half * channels, (half + 1) * channels)
+            parts.append(
+                prepare(
+                    values, dec_member, 2 * channels // GROUPS, gd[:, lanes], od[:, lanes], dec_cols.at[image],
+                    side, 2 * channels, half * channels,
+                )
+            )
+        while parts:
+            for part in tuple(parts):
+                try:
+                    next(part)
+                except StopIteration:
+                    parts.remove(part)
+            yield
+
+    def convolve(is_enc, tick, image):
+        step = tick * images + image
+        if is_enc:
+            return conv_add(
+                encoded, enc_pack, step, enc_cols.at[image], we, enc_tail, False, enc_source(tick, image), be[...], side
+            )
+        return conv_add(
+            decoded, dec_pack, step, dec_cols.at[image], wd, dec_tail, True, dec_source(tick, image), bd[...], side
+        )
+
+    def send(is_enc, tick, image):
+        if is_enc:
             if tick == 0 and image == 0:
                 pl.semaphore_wait(barrier, 1)
                 if sections > 2:
@@ -232,39 +284,39 @@
                 def _():
                     enc_next(tick, image).start()
 
-        for image in range(images):
-            if tick == 0 and image == 0:
-                for copy in loads[5:9]:
-                    copy.wait()
-            place = span(tick, image)
-            skipped = sk[place, :].astype(F32)
-            if tick == 0:
-                current = d0[image * rows : (image + 1) * rows, :].astype(F32)
-            else:
-
-                @pl.when(me > 0)
-                def _():
-                    dec_next(tick - 1, image).wait_recv()
-
-                moved = joined(q_buf, tick - 1, image)
-                current = jnp.where(me == 0, moved, joined(d_buf, tick - 1, image))
-                skipped = jnp.where(me == 0, moved, skipped)
-            for half, values in enumerate((current, skipped)):
-                lanes = slice(half * channels, (half + 1) * channels)
-                hidden = norm_silu(values, dec_member, 2 * channels // GROUPS, gd[:, lanes], od[:, lanes])
-                spread(dec_cols.at[image], hidden, side, 2 * channels, half * channels)
-            if tick == 0 and image == 0:
-                for copy in loads[9:10] + loads[11:]:
-                    copy.wait()
-            conv_add(
-                decoded, dec_pack, tick * images + image, dec_cols.at[image], wd, dec_tail, True, current, bd[...],
-                side,
-            )
-            if tick < ticks - 1:
-
-                @pl.when(me < sections - 1)
-                def _():
-                    dec_next(tick, image).start()
+        elif tick < ticks - 1:
+
+            @pl.when(me < sections - 1)
+            def _():
+                dec_next(tick, image).start()
+
+    stages = [
+        (is_enc, tick, image) for tick in range(ticks) for is_enc in (True, False) for image in range(images)
+    ]
+    enc_member = membership(channels, channels // GROUPS)
+    clear(enc_cols)
+    for copy in loads[:3]:
+        copy.wait()
+    weave(ready(*stages[0]))
+    for copy in loads[3:5]:
+        copy.wait()
+    for copy in loads[5:]:
+        copy.start()
+    for tap in range(3):
+        enc_tail[:, tap * narrow : (tap + 1) * narrow] = we[tap, :, wide:]
+    dec_member = None
+    for index, stage in enumerate(stages):
+        following = stages[index + 1 : index + 2]
+        for coming in following:
+            arrive(*coming)
+            if dec_member is None and not coming[0]:
+                dec_member = membership(channels, 2 * channels // GROUPS)
+                clear(dec_cols)
+        if stage == (False, 0, 0):
+            for copy in loads[9:10] + loads[11:]:
+                copy.wait()
+        weave(convolve(*stage), *[ready(*coming) for coming in following])
+        send(*stage)
 
     for image in range(images):
         to_mirror(ticks - 1, image).wait_recv()

time: 28.2 us -> 28.3 us (level)
  no operation moved by 1% of the time
where the time goes in v4:
time: 28.3 us; the launch traced here: 28.1 us
  Pallas kernels  27.5 us (97%)
  between operations  0.64 us (2%)
    pallas_call x1, Pallas kernels, shards(): pl.pallas_call(functools.partial(relay, sections, ticks, images, side), o...  26 us
    pallas_call x1, Pallas kernels, shards(): pl.pallas_call(hand_on, out_shape=(maps, maps, maps), in_specs=[anywhere]...  1.45 us

profile of v4, /device:TPU:10, one launch (start us, length us, event | category | flops | bytes accessed | tf_op | source)
XLA Modules:
  0.0 28.1 jit_solution(9096699408151985235)
XLA Ops:
  0.6 26.0 %shard_map.139 = (bf16[1024,320]{1,0:T(8,128)(2,1)S(1)}, bf16[1024,320]{1,0:T(8,128)(2,1)S(1)}, bf16[1024,320]{1,0:T(8,128)(2,1)S(1)}) custom-call(bf16[512,320]{1,0:T(8,128)(2,1)} %bitcast.17, bf16[512,320]{1,0:T(8,128)(2,1)} %bitcast.18, bf16[512,320]{1,0:T(8,128)(2,1)} %bitcast.19, bf16[1024,320]{1,0:T(8,128)(2,1)} %bitcast.13, ...), custom_call_target="tpu_custom_call" | custom-call | flops 5662310400 | bytes 12582912 | tf_op jit(solution)/shard_map/pallas_call | solution.py:380
  26.7 1.4 %shard_map.140 = (bf16[1024,320]{1,0:T(8,128)(2,1)}, bf16[1024,320]{1,0:T(8,128)(2,1)}, bf16[1024,320]{1,0:T(8,128)(2,1)}) custom-call(bf16[1024,320]{1,0:T(8,128)(2,1)S(1)} %get-tuple-element.9.refs_0_, bf16[1024,320]{1,0:T(8,128)(2,1)S(1)} %get-tuple-element.10.refs_1_, bf16[1024,320]{1,0:T(8,128)(2,1)S(1)} %get-tuple-element.11.refs_2_), custom_call_target="tpu_custom_call" | custom-call | tf_op jit(solution)/shard_map/pallas_call | solution.py:406

commit v5 on v4

--- a/solution.py
+++ b/solution.py
@@ -8,6 +8,7 @@
 from jax.sharding import PartitionSpec as P
 
 GROUPS = 32
+STRIPS = 2
 LANES = 256
 F32 = jnp.float32
 BF16 = jnp.bfloat16
@@ -83,27 +84,33 @@
     return source[start : start + rows, :], jnp.concatenate(tail, axis=0)
 
 
-def conv_add(out, packed, step, buffer, weight, tail, flipped, source, bias, side):
-    rows, width = source.shape
-    start = step * rows
+def conv_add(out, packed, step, buffer, weight, tail, flipped, source, bias, side, strips):
+    strip = source.shape[0] // STRIPS
+    first, rows = strips[0] * strip, len(strips) * strip
+    start = step * source.shape[0] + first
+    block = packed.shape[0] * strip // out.shape[0]
+    source = source[first : first + rows, :]
+    width = source.shape[1]
     wide = width // LANES * LANES
     narrow = width - wide
     total = source[:, :wide] + bias[:, :wide]
     for tap in range(3):
         total += product(
-            buffer[tap * side : tap * side + rows, :], weight[tap] if flipped else weight[tap, :, :wide], flipped
+            buffer[first + tap * side : first + tap * side + rows, :], weight[tap] if flipped else weight[tap, :, :wide], flipped
         )
         yield
     main = total.astype(BF16)
     out[start : start + rows, :wide] = main
-    ends = product(buffer[...], tail[...], flipped)
+    ends = product(buffer[first : first + rows + 2 * side, :], tail[...], flipped)
     yield
     total = source[:, wide:] + bias[:, wide:]
     for tap in range(3):
         total += ends[tap * side : tap * side + rows, tap * narrow : (tap + 1) * narrow]
     rest = total.astype(BF16)
     out[start : start + rows, wide:] = rest
-    pack(packed, step * packed.shape[0] // (out.shape[0] // rows), main, rest)
+    for place, part in enumerate(strips):
+        lines = slice(place * strip, (place + 1) * strip)
+        pack(packed, (step * STRIPS + part) * block, main[lines], rest[lines])
 
 
 def relay(sections, ticks, images, side, *refs):
@@ -153,7 +160,11 @@
         return pl.ds((tick * images + image) * packed, packed)
 
     def opened(source, tick, image):
-        return unpack(source, (tick * images + image) * packed, rows, narrow)
+        start = (tick * images + image) * packed
+        parts = [
+            unpack(source, start + part * packed // STRIPS, rows // STRIPS, narrow) for part in range(STRIPS)
+        ]
+        return [jnp.concatenate(pieces, axis=0) for pieces in zip(*parts)]
 
     def joined(source, tick, image):
         return jnp.concatenate([part.astype(F32) for part in opened(source, tick, image)], axis=1)
@@ -165,14 +176,22 @@
         queued[start : start + rows, wide:] = rest
 
     def to_mirror(tick, image):
-        return pltpu.make_async_remote_copy(
-            src_ref=enc_pack.at[bundle(tick, image)],
-            dst_ref=q_buf.at[bundle(tick, image)],
-            send_sem=q_send.at[tick * images + image],
-            recv_sem=q_recv.at[tick * images + image],
-            device_id={"section": mirror},
-            device_id_type=MESH,
-        )
+        step = tick * images + image
+        pieces = [(step, step * packed, packed)]
+        if step == 0:
+            block = packed // STRIPS
+            pieces = [(part if part == 0 else ticks * images + part - 1, part * block, block) for part in range(STRIPS)]
+        return [
+            pltpu.make_async_remote_copy(
+                src_ref=enc_pack.at[pl.ds(start, size)],
+                dst_ref=q_buf.at[pl.ds(start, size)],
+                send_sem=q_send.at[slot],
+                recv_sem=q_recv.at[slot],
+                device_id={"section": mirror},
+                device_id_type=MESH,
+            )
+            for slot, start, size in pieces
+        ]
 
     def to_next(source, target, send, recv, tick, image):
         return pltpu.make_async_remote_copy(
@@ -218,7 +237,8 @@
         if is_enc:
             if tick == 1 and image == 0:
                 loads[10].wait()
-            to_mirror(tick - 1, image).wait_recv()
+            for copy in to_mirror(tick - 1, image):
+                copy.wait_recv()
             if sections > 2:
 
                 @pl.when(behind)
@@ -257,27 +277,22 @@
                     parts.remove(part)
             yield
 
-    def convolve(is_enc, tick, image):
+    def convolve(is_enc, tick, image, strips):
         step = tick * images + image
         if is_enc:
             return conv_add(
-                encoded, enc_pack, step, enc_cols.at[image], we, enc_tail, False, enc_source(tick, image), be[...], side
+                encoded, enc_pack, step, enc_cols.at[image], we, enc_tail, False, enc_source(tick, image), be[...],
+                side, strips,
             )
         return conv_add(
-            decoded, dec_pack, step, dec_cols.at[image], wd, dec_tail, True, dec_source(tick, image), bd[...], side
+            decoded, dec_pack, step, dec_cols.at[image], wd, dec_tail, True, dec_source(tick, image), bd[...],
+            side, strips,
         )
 
     def send(is_enc, tick, image):
         if is_enc:
-            if tick == 0 and image == 0:
-                pl.semaphore_wait(barrier, 1)
-                if sections > 2:
-
-                    @pl.when(ahead)
-                    def _():
-                        pl.semaphore_wait(barrier, 1)
-
-            to_mirror(tick, image).start()
+            for copy in to_mirror(tick, image)[-1:]:
+                copy.start()
             if sections > 2 and tick < ticks - 1:
 
                 @pl.when(ahead)
@@ -304,6 +319,17 @@
         copy.start()
     for tap in range(3):
         enc_tail[:, tap * narrow : (tap + 1) * narrow] = we[tap, :, wide:]
+    for part in range(STRIPS - 1):
+        weave(convolve(*stages[0], range(part, part + 1)))
+        if part == 0:
+            pl.semaphore_wait(barrier, 1)
+            if sections > 2:
+
+                @pl.when(ahead)
+                def _():
+                    pl.semaphore_wait(barrier, 1)
+
+        to_mirror(0, 0)[part].start()
     dec_member = None
     for index, stage in enumerate(stages):
         following = stages[index + 1 : index + 2]
@@ -315,15 +341,18 @@
         if stage == (False, 0, 0):
             for copy in loads[9:10] + loads[11:]:
                 copy.wait()
-        weave(convolve(*stage), *[ready(*coming) for coming in following])
+        strips = range(STRIPS) if index else range(STRIPS - 1, STRIPS)
+        weave(convolve(*stage, strips), *[ready(*coming) for coming in following])
         send(*stage)
 
     for image in range(images):
-        to_mirror(ticks - 1, image).wait_recv()
+        for copy in to_mirror(ticks - 1, image):
+            copy.wait_recv()
         keep_mirrored(ticks - 1, image)
     for tick in range(ticks):
         for image in range(images):
-            to_mirror(tick, image).wait_send()
+            for copy in to_mirror(tick, image):
+                copy.wait_send()
             if tick < ticks - 1:
                 if sections > 2:
 
@@ -340,9 +369,9 @@
     count = len(refs) // 2
     copies = []
     for source, target in zip(refs[:count], refs[count:-1]):
-        half = source.shape[0] // 2
-        for part in range(2):
-            at = pl.ds(part * half, half)
+        size = source.shape[0] // 4
+        for part in range(4):
+            at = pl.ds(part * size, size)
             copies.append(pltpu.make_async_copy(source.at[at], target.at[at], refs[-1].at[len(copies)]))
     for copy in copies:
         copy.start()
@@ -395,7 +424,7 @@
             pltpu.VMEM((3 * narrow, 6 * channels), BF16),
             pltpu.SemaphoreType.DMA((len(operands) + 17,)),
         ]
-        + [pltpu.SemaphoreType.DMA((steps,))] * 6,
+        + [pltpu.SemaphoreType.DMA((steps + STRIPS - 1,))] * 6,
         compiler_params=pltpu.CompilerParams(
             collective_id=0, has_side_effects=True, vmem_limit_bytes=56 * 1024 * 1024
         ),
@@ -408,7 +437,7 @@
         out_shape=(maps, maps, maps),
         in_specs=[anywhere] * 3,
         out_specs=[anywhere] * 3,
-        scratch_shapes=[pltpu.SemaphoreType.DMA((6,))],
+        scratch_shapes=[pltpu.SemaphoreType.DMA((12,))],
         compiler_params=pltpu.CompilerParams(vmem_limit_bytes=4 * 1024 * 1024),
     )(*outs)
     return tuple(out.reshape(ticks * images, side, side, channels) for out in outs)

time: 28.3 us -> 27.6 us (0.975)
  Pallas kernels: 27.5 us -> 26.8 us
    pallas_call x1, Pallas kernels: 26 us -> 25.4 us  [shards(): pl.pallas_call(functools.partial(relay, sections, ticks, images, side), o...]
where the time goes in v5:
time: 27.6 us; the launch traced here: 27.5 us
  Pallas kernels  26.8 us (97%)
  between operations  0.64 us (2%)
    pallas_call x1, Pallas kernels, shards(): pl.pallas_call(functools.partial(relay, sections, ticks, images, side), o...  25.4 us
    pallas_call x1, Pallas kernels, shards(): pl.pallas_call(hand_on, out_shape=(maps, maps, maps), in_specs=[anywhere]...  1.49 us

profile of v5, /device:TPU:10, one launch (start us, length us, event | category | flops | bytes accessed | tf_op | source)
XLA Modules:
  0.0 27.5 jit_solution(448439048558463447)
XLA Ops:
  0.6 25.4 %shard_map.139 = (bf16[1024,320]{1,0:T(8,128)(2,1)S(1)}, bf16[1024,320]{1,0:T(8,128)(2,1)S(1)}, bf16[1024,320]{1,0:T(8,128)(2,1)S(1)}) custom-call(bf16[512,320]{1,0:T(8,128)(2,1)} %bitcast.17, bf16[512,320]{1,0:T(8,128)(2,1)} %bitcast.18, bf16[512,320]{1,0:T(8,128)(2,1)} %bitcast.19, bf16[1024,320]{1,0:T(8,128)(2,1)} %bitcast.13, ...), custom_call_target="tpu_custom_call" | custom-call | flops 5662310400 | bytes 12582912 | tf_op jit(solution)/shard_map/pallas_call | solution.py:409
  26.0 1.5 %shard_map.140 = (bf16[1024,320]{1,0:T(8,128)(2,1)}, bf16[1024,320]{1,0:T(8,128)(2,1)}, bf16[1024,320]{1,0:T(8,128)(2,1)}) custom-call(bf16[1024,320]{1,0:T(8,128)(2,1)S(1)} %get-tuple-element.9.refs_0_, bf16[1024,320]{1,0:T(8,128)(2,1)S(1)} %get-tuple-element.10.refs_1_, bf16[1024,320]{1,0:T(8,128)(2,1)S(1)} %get-tuple-element.11.refs_2_), custom_call_target="tpu_custom_call" | custom-call | tf_op jit(solution)/shard_map/pallas_call | solution.py:435
